TPU v7x, 32 devices: a whole 2x2x4 slice. The times are simulated.
32 devices in a mesh: dp: 4 (over y, x), expert: 8 (over z, core).
Axes of the slice: x: 2, y: 2, z: 4, core: 2. Of those that a mesh axis runs over, the one named last changes fastest.
Arguments:
- tokens: bfloat16 [1024, 4096], P('dp', 'expert'), may hold values from -6 to 6
- out_grads: bfloat16 [1024, 4096], P('dp', 'expert'), may hold values from -6 to 6
- routes: int32 [1024, 2], P('dp'), may hold values from 0 to 7, all different within a row; in each aligned block of 256 rows (0 to 255, 256 to 511, ...) at most 64 rows name the same one
- gate_codes: int32 [1024, 2], P('dp'), may hold values from 256 to 4095
- w_gate: bfloat16 [8, 4096, 6400], P('expert', None, 'dp'), may hold values from -0.09375 to 0.09375
- w_up: bfloat16 [8, 4096, 6400], P('expert', None, 'dp'), may hold values from -0.09375 to 0.09375
- w_down: bfloat16 [8, 6400, 4096], P('expert', 'dp'), may hold values from -0.078125 to 0.078125
- proj_in: bfloat16 [4096, 128], replicated, may hold values from -0.09375 to 0.09375
- proj_hidden: bfloat16 [6400, 192], P('dp'), may hold values from -0.078125 to 0.078125
Outputs:
- projected: float32 [4, 8, 12288], P(None, 'expert', 'dp')
Inputs may be any that keep to these rules, and one draw needn't show every extreme that they name: `routes`: each row names 2 different experts. Among the rows of one sequence no expert is named more than 64 times, a bound that some block reaches.
All inputs are finite; a program needn't handle non-finite values.
Results may differ from a plain program's by a relative error of at most 0.0029.
Values may be sent and summed in bfloat16 or wider, within the bound.
A program may use at most 128 MiB of HBM per device.

v0:
```python
import jax
import jax.numpy as jnp
from jax import lax
from jax.sharding import PartitionSpec as P


def slot_pack(x_rows, dy_rows, route_rows, code_rows, first_row, n_exp, cap, seq_len):
    count = x_rows.shape[0]
    flat = route_rows.reshape(-1)
    pairs = flat.shape[0]
    expert_ids = jnp.arange(n_exp, dtype=jnp.int32)
    hits = (flat[:, None] == expert_ids[None, :]).astype(jnp.float32)
    earlier = (jnp.arange(pairs)[None, :] < jnp.arange(pairs)[:, None]).astype(jnp.float32)
    before = jnp.dot(earlier, hits, preferred_element_type=jnp.float32)
    place = jnp.sum(hits * before, axis=1).astype(jnp.int32)
    slot_ids = jnp.arange(cap, dtype=jnp.int32)
    match = (
        (flat[:, None, None] == expert_ids[None, :, None])
        & (place[:, None, None] == slot_ids[None, None, :])
    ).astype(jnp.int32)
    row_match = match.reshape(count, route_rows.shape[1], n_exp, cap).sum(axis=1)
    picks = row_match.reshape(count, n_exp * cap).T.astype(jnp.bfloat16)
    x_slots = jnp.dot(picks, x_rows, preferred_element_type=jnp.float32).astype(jnp.bfloat16)
    dy_slots = jnp.dot(picks, dy_rows, preferred_element_type=jnp.float32).astype(jnp.bfloat16)
    slot_code = jnp.sum(match * code_rows.reshape(-1)[:, None, None], axis=0)
    seq_rows = (first_row + jnp.arange(count, dtype=jnp.int32)) // seq_len
    slot_seq = jnp.sum(row_match * (seq_rows[:, None, None] + 1), axis=0) - 1
    meta = jnp.stack([slot_code, slot_seq], axis=-1)
    width = x_rows.shape[1]
    return (x_slots.reshape(n_exp, cap, width), dy_slots.reshape(n_exp, cap, width), meta)


def expert_rows(xs, dys, meta, weights):
    wg, wu, wd, proj_in, proj_hidden = weights
    rank = proj_in.shape[1] // 2
    weight = meta[:, 0].astype(jnp.float32) / 4096.0
    gate = jnp.dot(xs, wg, preferred_element_type=jnp.float32)
    upper = jnp.dot(xs, wu, preferred_element_type=jnp.float32)
    sig = jax.nn.sigmoid(gate)
    act = gate * sig
    hidden = (act * upper).astype(jnp.bfloat16)
    back = (
        lax.dot_general(dys, wd, (((1,), (1,)), ((), ())), preferred_element_type=jnp.float32)
        * weight[:, None]
    )
    d_up = (back * act).astype(jnp.bfloat16)
    d_gate = (back * upper * sig * (1.0 + gate * (1.0 - sig))).astype(jnp.bfloat16)
    in_proj = jnp.dot(xs, proj_in[:, :rank], preferred_element_type=jnp.float32)
    out_proj = jnp.dot(dys, proj_in[:, rank:], preferred_element_type=jnp.float32) * weight[:, None]
    hid_proj = jnp.dot(hidden, proj_hidden[:, :rank], preferred_element_type=jnp.float32)
    gate_proj = jnp.dot(d_gate, proj_hidden[:, rank : 2 * rank], preferred_element_type=jnp.float32)
    up_proj = jnp.dot(d_up, proj_hidden[:, 2 * rank :], preferred_element_type=jnp.float32)
    return jnp.concatenate([in_proj, out_proj, hid_proj, gate_proj, up_proj], axis=1)


def kron_sums(rows, meta, n_seq):
    rank = rows.shape[1] // 5
    in_proj = rows[:, :rank]
    out_proj = rows[:, rank : 2 * rank]
    hid_proj = rows[:, 2 * rank : 3 * rank]
    gate_proj = rows[:, 3 * rank : 4 * rank]
    up_proj = rows[:, 4 * rank :]
    onehot = (meta[:, 1:2] == jnp.arange(n_seq, dtype=jnp.int32)[None, :]).astype(jnp.float32)
    lefts = jnp.stack([in_proj, in_proj, hid_proj])
    rights = jnp.stack([gate_proj, up_proj, out_proj])
    total = jnp.einsum("ns,knr,knq->skrq", onehot, lefts, rights, precision=lax.Precision.HIGHEST)
    return total.reshape(n_seq, 3 * rank * rank)


def column_rows(xs, dys, meta, weights):
    return expert_rows(xs, dys, meta, weights)


def per_device(tokens, out_grads, routes, gate_codes, w_gate, w_up, w_down, proj_in, proj_hidden):
    n_dp = lax.axis_size("dp")
    n_exp = lax.axis_size("expert")
    rows_here = tokens.shape[0]
    cap = rows_here // 4
    mine = lax.axis_index("expert")
    weights = (w_gate[0], w_up[0], w_down[0], proj_in, proj_hidden)
    first_row = lax.axis_index("dp") * rows_here
    x_slots, dy_slots, meta_all = slot_pack(
        tokens, out_grads, routes, gate_codes, first_row, n_exp, cap, rows_here
    )
    x_slots, dy_slots = (
        lax.all_to_all(x_slots, "expert", split_axis=0, concat_axis=2, tiled=True),
        lax.all_to_all(dy_slots, "expert", split_axis=0, concat_axis=2, tiled=True),
    )
    width = x_slots.shape[2]
    x_slots = x_slots.reshape(cap, width)
    dy_slots = dy_slots.reshape(cap, width)
    meta = lax.dynamic_index_in_dim(meta_all, mine, 0, keepdims=False)
    piece = (
        lax.all_gather(x_slots, "dp", axis=0, tiled=True),
        lax.all_gather(dy_slots, "dp", axis=0, tiled=True),
        lax.all_gather(meta, "dp", axis=0, tiled=True),
    )
    values = column_rows(piece[0], piece[1], piece[2], weights)
    partial_sums = kron_sums(values, piece[2], n_dp)
    share = lax.psum_scatter(partial_sums, "dp", scatter_dimension=1, tiled=True)
    return share.reshape(n_dp, 1, share.shape[1])


def solution(mesh):
    return jax.shard_map(
        per_device,
        mesh=mesh,
        in_specs=(
            P("dp", "expert"),
            P("dp", "expert"),
            P("dp", None),
            P("dp", None),
            P("expert", None, "dp"),
            P("expert", None, "dp"),
            P("expert", "dp", None),
            P(),
            P("dp", None),
        ),
        out_specs=P(None, "expert", "dp"),
        check_vma=False,
    )
```

profile of v0, /device:TPU:0, one launch (start us, length us, event | category | flops | bytes accessed | tf_op | source)
XLA Modules:
  0.0 209.4 jit_solution(6605572059555730455)
XLA Ops:
  6.5 0.0 copy-start
  6.5 0.0 all-gather.4.cloned.1.call-start
  6.5 0.7 iota_compare_fusion.5
  7.3 0.8 copy.37
  8.1 0.1 eq.77
  8.2 0.3 fusion.11
  8.5 0.1 convert_element_type.45
  8.7 0.1 copy.38
  8.8 0.1 convert_reduce_fusion
  8.9 0.2 fusion.36
  9.1 0.0 copy-done
  9.1 0.0 copy-start.4
  9.1 0.3 convolution_convert_fusion.1
  9.4 21.5 %all_to_all.30 = bf16[8,64,512]{2,1,0:T(8,128)(2,1)S(1)} all-to-all(bf16[8,64,512]{2,1,0:T(8,128)(2,1)S(1)} %bitcast.78), channel_id=1, replica_groups=mesh['dp'=4,'expert'=8] {'expert'}, dimensions={0} | all-to-all | bytes 1048576 | tf_op jit(solution)/shard_map/all_to_all | solution.py:86
  30.9 0.8 copy.50
  31.8 0.0 all-gather.4.cloned.1.call-update
  31.8 0.0 copy-start.5
  31.8 0.0 all-gather.6.cloned.1.call-start
  31.9 0.0 copy-done.4
  31.9 0.3 convolution_convert_fusion
  32.2 17.8 %all_to_all.31 = bf16[8,64,512]{2,1,0:T(8,128)(2,1)S(1)} all-to-all(bf16[8,64,512]{2,1,0:T(8,128)(2,1)S(1)} %bitcast.76), channel_id=1, replica_groups=mesh['dp'=4,'expert'=8] {'expert'}, dimensions={0} | all-to-all | bytes 1048576 | tf_op jit(solution)/shard_map/all_to_all | solution.py:87
  49.9 0.9 copy.51
  50.8 0.0 all-gather.6.cloned.1.call-update
  50.8 0.0 reduce-scatter.4.cloned.1.call-start
  50.9 0.0 copy-done.5
  50.9 0.1 copy.40
  51.0 0.1 mul.66
  51.2 0.2 select_reduce_fusion
  51.5 0.1 copy.41
  51.6 9.6 %all-gather = s32[1,256,2]{2,0,1:T(1,128)S(1)} all-gather(s32[1,64,2]{2,0,1:T(1,128)S(1)} %copy.41), channel_id=2, replica_groups=mesh['dp'=4,'expert'=8] {'dp'}, dimensions={1}, use_global_device_ids=true | all-gather | bytes 2560 | tf_op jit(solution)/shard_map/all_gather | solution.py:96
  61.2 0.2 slice_reduce_fusion
  61.4 0.1 fusion.28
  61.5 5.7 %all-gather.4.cloned.1.call-done = bf16[256,4096]{1,0:T(8,128)(2,1)} async-done(((bf16[64,4096]{1,0:T(8,128)(2,1)}), bf16[256,4096]{1,0:T(8,128)(2,1)}) %all-gather.4.cloned.1.call-update) | async-done | bytes 2097168 | tf_op jit(solution)/shard_map/all_gather | solution.py:94
  67.2 7.3 %fusion.4 = f32[256,1600]{0,1:T(8,128)S(1)} fusion(bf16[256,4096]{1,0:T(8,128)(2,1)} %all-gather.4.cloned.1.call-done, bf16[1,4096,1600]{1,2,0:T(8,128)(2,1)} %param.13), kind=kOutput, calls=%fused_computation.4 | convolution fusion | flops 3355443200 | bytes 16842752 | tf_op jit(solution)/shard_map/dot_general | solution.py:37
  74.5 0.0 copy-start.6
  74.5 29.9 %all-gather.6.cloned.1.call-done = bf16[256,4096]{1,0:T(8,128)(2,1)} async-done(((bf16[64,4096]{1,0:T(8,128)(2,1)}), bf16[256,4096]{1,0:T(8,128)(2,1)}) %all-gather.6.cloned.1.call-update) | async-done | bytes 2097168 | tf_op jit(solution)/shard_map/all_gather | solution.py:95
  104.4 7.3 %fusion.6 = f32[256,1600]{0,1:T(8,128)S(1)} fusion(bf16[256,4096]{1,0:T(8,128)(2,1)} %all-gather.6.cloned.1.call-done, bf16[1,1600,4096]{2,1,0:T(8,128)(2,1)} %param.15, f32[256]{0:T(256)S(1)} %fusion.28), kind=kOutput, calls=%fused_computation.6 | convolution fusion | flops 3355852800 | bytes 16843776 | tf_op jit(solution)/shard_map/dot_general | solution.py:43
  111.7 0.0 copy-done.6
  111.8 0.0 copy-start.2
  111.8 0.6 convolution_bitcast_fusion.1
  112.3 1.0 copy-done.2
  113.4 6.7 %fusion.2 = f32[256,1600]{0,1:T(8,128)S(1)} fusion(bf16[256,4096]{1,0:T(8,128)(2,1)S(1)} %copy-done.2, bf16[1,4096,1600]{1,2,0:T(8,128)(2,1)} %param.14), kind=kOutput, calls=%fused_computation.2 | convolution fusion | flops 3355443200 | bytes 16842752 | tf_op jit(solution)/shard_map/dot_general | solution.py:38
  120.0 0.7 convolution_bitcast_fusion.2
  120.8 0.0 copy-start.1
  120.8 0.6 convolution_bitcast_fusion.3
  121.4 0.6 copy-done.1
  122.0 0.0 copy-start.3
  122.0 0.8 convolution_bitcast_fusion.4
  122.8 0.8 copy-done.3
  123.6 1.3 fusion.10
  125.0 0.8 convolution_bitcast_fusion
  125.8 4.2 %copy.48 = f32[4,3,64,64]{0,3,2,1:T(8,128)} copy(f32[4,3,64,64]{3,2,0,1:T(8,128)S(1)} %convolution_bitcast_fusion) | data formatting | bytes 393216
  129.9 0.0 reduce-scatter.4.cloned.1.call-update
  129.9 70.4 %reduce-scatter.4.cloned.1.call-done = f32[3072,4]{1,0:T(8,128)} async-done(((f32[12288,4]{1,0:T(8,128)}), f32[3072,4]{1,0:T(8,128)}) %reduce-scatter.4.cloned.1.call-update) | async-done | bytes 49168
  200.3 1.9 copy.47
  202.2 0.7 copy.44
  (9 shorter events, 0.1 us)
Async XLA Ops:
  6.5 2.6 %copy-start = (bf16[256,512]{1,0:T(8,128)(2,1)S(1)}, bf16[256,512]{1,0:T(8,128)(2,1)}, u32[]{:S(2)}) copy-start(bf16[256,512]{1,0:T(8,128)(2,1)} %param.9) | copy-start | bytes 786436
  6.5 60.7 %all-gather.4.cloned.1.call-start = ((), (), s32[]{:S(2)}) async-start(), calls=%async_computation.3 | async-start | bytes 2621440 | tf_op jit(solution)/shard_map/all_gather | solution.py:94
  9.1 22.7 %copy-start.4 = (bf16[256,512]{1,0:T(8,128)(2,1)S(1)}, bf16[256,512]{1,0:T(8,128)(2,1)}, u32[]{:S(2)}) copy-start(bf16[256,512]{1,0:T(8,128)(2,1)} %param.10) | copy-start | bytes 786436
  31.8 19.1 %copy-start.5 = (s32[256,2]{0,1:T(2,128)S(1)}, s32[256,2]{0,1:T(2,128)}, u32[]{:S(2)}) copy-start(s32[256,2]{0,1:T(2,128)} %param.12) | copy-start | bytes 6148
  31.8 72.6 %all-gather.6.cloned.1.call-start = ((), (), s32[]{:S(2)}) async-start(), calls=%async_computation.4 | async-start | bytes 2621440 | tf_op jit(solution)/shard_map/all_gather | solution.py:95
  50.8 149.5 %reduce-scatter.4.cloned.1.call-start = ((), (), s32[]{:S(2)}) async-start(), calls=%async_computation.5 | async-start | bytes 7864320
  74.5 37.2 %copy-start.6 = (bf16[1600,192]{0,1:T(8,128)(2,1)S(1)}, bf16[1600,192]{0,1:T(8,128)(2,1)}, u32[]{:S(2)}) copy-start(bf16[1600,192]{0,1:T(8,128)(2,1)} %param.17) | copy-start | bytes 1843204
  111.8 1.6 copy-start.2
  120.8 1.2 copy-start.1
  122.0 1.6 copy-start.3
Sparse Core Ops, SparseCore 0:
  31.9 35.2 all-gather.3
  69.1 35.3 all-gather.5
  130.1 70.2 reduce-scatter.3
where the time goes:
time: 210 us; the launch traced here: 209 us
  waiting for transfers between devices  106 us (50%)
  blocking collectives  48.9 us (23%)
  matrix products  26.9 us (13%)
  between operations  13.4 us (6%)
  local copies, waits for them, and re-layouts  12.6 us (6%)
    unnamed x4, waiting for transfers between devices  70.4 us
    all_gather x1, waiting for transfers between devices, per_device(): lax.all_gather(dy_slots, 'dp', axis=0, tiled=True)  29.9 us
    all_to_all x1, blocking collectives, per_device(): lax.all_to_all(x_slots, 'expert', split_axis=0, concat_axis=2, tiled=True)  21.5 us
    all_to_all x1, blocking collectives, per_device(): lax.all_to_all(dy_slots, 'expert', split_axis=0, concat_axis=2, tiled=True)  17.8 us
    unnamed x20, local copies, waits for them, and re-layouts  11.1 us
    all_gather x1, blocking collectives, per_device(): lax.all_gather(meta, 'dp', axis=0, tiled=True)  9.62 us
    dot_general x1, matrix products, expert_rows(): lax.dot_general(dys, wd, (((1,), (1,)), ((), ())), preferred_element_type...  7.31 us
    dot_general x1, matrix products, expert_rows(): gate = jnp.dot(xs, wg, preferred_element_type=jnp.float32)  7.29 us
  transfers between devices with their start and end apart: 3, of which 3 were waited for; matrix products, arithmetic and copies ran while one was open for 4% of the time, Pallas kernels for 0%

commit v1 on v0

v1 whole, which is shorter than its diff:
```python
import functools
import math

import jax
import jax.numpy as jnp
from jax import lax
from jax.experimental import pallas as pl
from jax.experimental.pallas import tpu as pltpu
from jax.sharding import PartitionSpec as P

MESH = pl.DeviceIdType.MESH
TILE = 256
LAG = 3


def swapped(a, b, count):
    total, bit = 0, 1
    while bit < count:
        total = total + lax.rem(lax.div(a, bit) + lax.div(b, bit), 2) * bit
        bit *= 2
    return total


def kernel(
    n_dp, n_exp, tokens, grads, routes, codes, w_gate, w_up, w_down, proj_in, proj_hidden, out,
    packed, slots, gate_w, up_w, down_w, gate, upper, back, in_sum, out_sum, hid_sum, weight_rows, parts, arrived,
    load_sem, send_one, recv_one, send_two, recv_two, recv_three, send_row, recv_row, send_part, recv_part,
):
    rows, chunk = tokens.shape
    cap = packed.shape[1]
    hidden = gate.shape[1]
    rank = proj_in.shape[1] // 2
    side = math.isqrt(n_dp)
    units = 2 * n_exp
    total_rows = n_dp * cap
    seq = lax.axis_index("dp")
    mine = lax.axis_index("expert")
    seq_y, seq_x = lax.div(seq, side), lax.rem(seq, side)

    def at_seq(index):
        return lax.rem(seq + index, n_dp)

    barrier = pltpu.get_barrier_semaphore()
    for step in range(1, n_dp):
        pl.semaphore_signal(barrier, inc=1, device_id=(at_seq(step), mine), device_id_type=MESH)
    for step in range(1, n_exp):
        pl.semaphore_signal(
            barrier, inc=1, device_id=(seq, lax.rem(mine + step, n_exp)), device_id_type=MESH
        )

    def weight_copy(which, j):
        span = pl.ds(pl.multiple_of(j * chunk, chunk), chunk)
        if which == 0:
            return pltpu.make_async_copy(w_gate.at[0, span, :], gate_w.at[j], load_sem.at[0, j])
        if which == 1:
            return pltpu.make_async_copy(w_up.at[0, span, :], up_w.at[j], load_sem.at[1, j])
        return pltpu.make_async_copy(w_down.at[0, :, span], down_w.at[j], load_sem.at[2, j])

    def load_x(k, carry):
        j = swapped(mine, k, n_exp)
        weight_copy(0, j).start()
        weight_copy(1, j).start()
        return carry

    def load_dy(k, carry):
        weight_copy(2, swapped(mine, k, n_exp)).start()
        return carry

    lax.fori_loop(0, n_exp, load_x, 0)
    lax.fori_loop(0, n_exp, load_dy, 0)

    lanes = max(128, n_exp)
    experts = lax.broadcasted_iota(jnp.int32, (rows, lanes), 1)
    first, second = routes[:, 0:1], routes[:, 1:2]
    hit = jnp.where((first == experts) | (second == experts), 1.0, 0.0)
    earlier = jnp.where(
        lax.broadcasted_iota(jnp.int32, (rows, rows), 1) < lax.broadcasted_iota(jnp.int32, (rows, rows), 0), 1.0, 0.0
    )
    place = jnp.dot(
        earlier.astype(jnp.bfloat16), hit.astype(jnp.bfloat16), preferred_element_type=jnp.float32
    )
    key = jnp.where(hit > 0.5, place, -1.0)
    keys = key.T
    slot_ids = lax.broadcasted_iota(jnp.int32, (cap, rows), 0).astype(jnp.float32)
    picks = jnp.concatenate(
        [jnp.where(keys[e : e + 1, :] == slot_ids, 1.0, 0.0).astype(jnp.bfloat16) for e in range(n_exp)], axis=0
    )
    for a, source in enumerate((tokens, grads)):
        values = jnp.dot(picks, source[...], preferred_element_type=jnp.float32).astype(jnp.bfloat16)
        packed[a * n_exp : (a + 1) * n_exp] = values.reshape(n_exp, cap, chunk)
        slots[a * n_exp + mine, seq] = packed[a * n_exp + mine]

    own_key = jnp.sum(jnp.where(experts == mine, key, 0.0), axis=1, keepdims=True)
    own_code = jnp.where(first == mine, codes[:, 0:1], 0) + jnp.where(second == mine, codes[:, 1:2], 0)
    slot_lanes = lax.broadcasted_iota(jnp.int32, (rows, 128), 1).astype(jnp.float32)
    own_weight = own_code.astype(jnp.float32) / 4096.0
    row = jnp.sum(jnp.where(own_key == slot_lanes, own_weight, 0.0), axis=0, keepdims=True)
    weight_rows[seq] = jnp.broadcast_to(row, (8, 128))

    pl.semaphore_wait(barrier, n_dp - 1 + n_exp - 1)

    def send_block(src, dst, send_sem, recv_sem, to_seq, to_expert):
        pltpu.make_async_remote_copy(
            src_ref=src, dst_ref=dst, send_sem=send_sem, recv_sem=recv_sem,
            device_id=(to_seq, to_expert), device_id_type=MESH,
        ).start()

    def wait_for(ref, sem):
        pltpu.make_async_copy(ref, ref, sem).wait()

    def peers(k):
        odd = lax.rem(k, 2)
        one, two = [], []
        for step in range(1, side):
            along_x = seq_y * side + lax.rem(seq_x + step, side)
            along_y = lax.rem(seq_y + step, side) * side + seq_x
            one.append(along_x + odd * (along_y - along_x))
            two.append(along_y + odd * (along_x - along_y))
        return one, two

    def split(unit):
        a, k = lax.div(unit, n_exp), lax.rem(unit, n_exp)
        return a, k, a * n_exp + swapped(mine, k, n_exp)

    def send_out(a):
        def body(k, carry):
            to = swapped(mine, k, n_exp)
            send_block(
                packed.at[a * n_exp + to], slots.at[a * n_exp + mine, seq],
                send_one, recv_one.at[a * n_exp + mine], seq, to,
            )
            return carry
        return body

    def stage_one(unit):
        a, k, at = split(unit)

        @pl.when(k > 0)
        def _():
            wait_for(slots.at[at, seq], recv_one.at[at])

        one, two = peers(k)
        for to in one:
            send_block(slots.at[at, seq], slots.at[at, seq], send_two, recv_two.at[at], to, mine)
        for to in two:
            send_block(slots.at[at, seq], slots.at[at, seq], send_two, recv_three.at[at], to, mine)

    def stage_two(unit):
        a, k, at = split(unit)
        one, two = peers(k)
        wait_for(slots.at[at, pl.ds(0, side - 1)], recv_two.at[at])
        for source in one:
            for to in two:
                send_block(slots.at[at, source], slots.at[at, source], send_two, recv_three.at[at], to, mine)

    def tiles():
        return [(n, min(TILE, hidden - n)) for n in range(0, hidden, TILE)]

    def stage_three(unit):
        a, k, at = split(unit)
        j = swapped(mine, k, n_exp)
        wait_for(slots.at[at, pl.ds(0, side * (side - 1))], recv_three.at[at])
        span = pl.ds(pl.multiple_of(j * chunk, chunk), chunk)

        @pl.when(a == 0)
        def _():
            weight_copy(0, j).wait()
            weight_copy(1, j).wait()
            block = slots[at].reshape(total_rows, chunk)
            in_sum[...] += jnp.dot(block, proj_in[span, :], preferred_element_type=jnp.float32)
            for n, width in tiles():
                cols = slice(n, n + width)
                gate[:, cols] += jnp.dot(block, gate_w[j, :, cols], preferred_element_type=jnp.float32)
                upper[:, cols] += jnp.dot(block, up_w[j, :, cols], preferred_element_type=jnp.float32)

        @pl.when(a == 1)
        def _():
            weight_copy(2, j).wait()
            block = slots[at].reshape(total_rows, chunk)
            out_sum[...] += jnp.dot(block, proj_in[span, :], preferred_element_type=jnp.float32)
            for n, width in tiles():
                cols = slice(n, n + width)
                back[:, cols] += lax.dot_general(
                    block, down_w[j, cols, :], (((1,), (1,)), ((), ())), preferred_element_type=jnp.float32
                )

        @pl.when(unit == n_exp - 1)
        def _():
            for n, width in tiles():
                cols = slice(n, n + width)
                g, u = gate[:, cols], upper[:, cols]
                sig = jax.nn.sigmoid(g)
                act = g * sig
                hid_sum[...] += jnp.dot(
                    (act * u).astype(jnp.bfloat16), proj_hidden[cols, :rank], preferred_element_type=jnp.float32
                )
                gate[:, cols] = act
                upper[:, cols] = u * sig * (1.0 + g * (1.0 - sig))

    lax.fori_loop(1, n_exp, send_out(0), 0)
    for step in range(1, n_dp):
        send_block(weight_rows.at[seq], weight_rows.at[seq], send_row, recv_row, at_seq(step), mine)
    lax.fori_loop(1, n_exp, send_out(1), 0)
    for ref in (gate, upper, back, in_sum, out_sum, hid_sum):
        ref[...] = jnp.zeros_like(ref)

    def body(step, carry):
        pl.when(step < units)(lambda: stage_one(step))
        pl.when((step >= 1) & (step <= units))(lambda: stage_two(step - 1))
        pl.when(step >= LAG)(lambda: stage_three(step - LAG))
        return carry

    lax.fori_loop(0, units + LAG, body, 0)

    wait_for(weight_rows.at[pl.ds(0, n_dp - 1)], recv_row)
    diagonal = lax.broadcasted_iota(jnp.int32, (cap, 128), 0) == lax.broadcasted_iota(jnp.int32, (cap, 128), 1)
    weight = jnp.concatenate(
        [
            jnp.sum(jnp.where(diagonal, weight_rows[s, 0:1, :], 0.0), axis=1, keepdims=True)
            for s in range(n_dp)
        ],
        axis=0,
    )
    gate_proj = jnp.zeros((total_rows, rank), jnp.float32)
    up_proj = jnp.zeros((total_rows, rank), jnp.float32)
    for n, width in tiles():
        cols = slice(n, n + width)
        scaled = back[:, cols] * weight
        up_proj += jnp.dot(
            (scaled * gate[:, cols]).astype(jnp.bfloat16), proj_hidden[cols, 2 * rank :],
            preferred_element_type=jnp.float32,
        )
        gate_proj += jnp.dot(
            (scaled * upper[:, cols]).astype(jnp.bfloat16), proj_hidden[cols, rank : 2 * rank],
            preferred_element_type=jnp.float32,
        )
    in_proj = in_sum[:, :rank]
    out_proj = out_sum[:, rank:] * weight
    hid_proj = hid_sum[...]
    share = 3 * rank // n_dp

    def product(left, right):
        return lax.dot_general(
            left, right, (((0,), (0,)), ((), ())),
            preferred_element_type=jnp.float32, precision=lax.Precision.HIGHEST,
        )

    for s in range(n_dp):
        part = slice(s * cap, (s + 1) * cap)
        stacked = jnp.concatenate(
            [
                product(in_proj[part], gate_proj[part]),
                product(in_proj[part], up_proj[part]),
                product(hid_proj[part], out_proj[part]),
            ],
            axis=0,
        )
        for d in range(n_dp):
            parts[d, s] = stacked[d * share : (d + 1) * share]
    for step in range(1, n_dp):
        to = at_seq(step)
        send_block(parts.at[to], arrived.at[seq], send_part, recv_part, to, mine)
    arrived[seq] = parts[seq]
    wait_for(arrived.at[pl.ds(0, n_dp - 1)], recv_part)
    result = arrived[0]
    for s in range(1, n_dp):
        result += arrived[s]
    out[...] = result

    wait_for(packed.at[pl.ds(0, 2 * (n_exp - 1))], send_one)
    wait_for(slots.at[:, pl.ds(0, n_dp - 1)], send_two)
    wait_for(weight_rows.at[pl.ds(0, n_dp - 1)], send_row)
    wait_for(parts.at[pl.ds(0, n_dp - 1)], send_part)


def per_device(tokens, out_grads, routes, gate_codes, w_gate, w_up, w_down, proj_in, proj_hidden):
    n_dp = lax.axis_size("dp")
    n_exp = lax.axis_size("expert")
    rows, chunk = tokens.shape
    cap = rows // 4
    hidden = w_gate.shape[2]
    rank = proj_in.shape[1] // 2
    share = 3 * rank // n_dp
    total = n_dp * cap
    vmem = pl.BlockSpec(memory_space=pltpu.VMEM)
    hbm = pl.BlockSpec(memory_space=pl.ANY)
    f32, bf16 = jnp.float32, jnp.bfloat16
    dma = pltpu.SemaphoreType.DMA
    result = pl.pallas_call(
        functools.partial(kernel, n_dp, n_exp),
        out_shape=jax.ShapeDtypeStruct((n_dp, share, rank), f32),
        in_specs=[vmem, vmem, vmem, vmem, hbm, hbm, hbm, vmem, vmem],
        out_specs=vmem,
        scratch_shapes=[
            pltpu.VMEM((2 * n_exp, cap, chunk), bf16),
            pltpu.VMEM((2 * n_exp, n_dp, cap, chunk), bf16),
            pltpu.VMEM((n_exp, chunk, hidden), bf16),
            pltpu.VMEM((n_exp, chunk, hidden), bf16),
            pltpu.VMEM((n_exp, hidden, chunk), bf16),
            pltpu.VMEM((total, hidden), f32),
            pltpu.VMEM((total, hidden), f32),
            pltpu.VMEM((total, hidden), f32),
            pltpu.VMEM((total, 2 * rank), f32),
            pltpu.VMEM((total, 2 * rank), f32),
            pltpu.VMEM((total, rank), f32),
            pltpu.VMEM((n_dp, 8, 128), f32),
            pltpu.VMEM((n_dp, n_dp, share, rank), f32),
            pltpu.VMEM((n_dp, n_dp, share, rank), f32),
            dma((3, n_exp)),
            dma, dma((2 * n_exp,)),
            dma, dma((2 * n_exp,)), dma((2 * n_exp,)),
            dma, dma,
            dma, dma,
        ],
        compiler_params=pltpu.CompilerParams(
            collective_id=0, has_side_effects=True, vmem_limit_bytes=60 * 1024 * 1024
        ),
    )(tokens, out_grads, routes, gate_codes, w_gate, w_up, w_down, proj_in, proj_hidden)
    return result.reshape(n_dp, 1, share * rank)


def solution(mesh):
    return jax.shard_map(
        per_device,
        mesh=mesh,
        in_specs=(
            P("dp", "expert"),
            P("dp", "expert"),
            P("dp", None),
            P("dp", None),
            P("expert", None, "dp"),
            P("expert", None, "dp"),
            P("expert", "dp", None),
            P(),
            P("dp", None),
        ),
        out_specs=P(None, "expert", "dp"),
        check_vma=False,
    )
```

time: 210 us -> 103 us (0.49)
  waiting for transfers between devices: 106 us -> 0 us
  Pallas kernels: 0 us -> 59.1 us
  blocking collectives: 48.9 us -> 0 us
  local copies, waits for them, and re-layouts: 12.6 us -> 42.6 us
  matrix products: 26.9 us -> 0 us
  between operations: 13.4 us -> 0.01 us
    unnamed x4 -> x0, waiting for transfers between devices: 70.4 us -> none
    pallas_call x0 -> x1, Pallas kernels: none -> 59.1 us  [per_device(): pl.pallas_call(functools.partial(kernel, n_dp, n_exp), out_shape=jax.Shap...]
    all_to_all x2 -> x0, blocking collectives: 39.3 us -> none  [the longest x1 21.5 us: per_device(): lax.all_to_all(x_slots, 'expert', split_axis=0, concat_axis=2, tiled=True)]
    all_gather x2 -> x0, waiting for transfers between devices: 35.6 us -> none  [the longest x1 29.9 us: per_device(): lax.all_gather(dy_slots, 'dp', axis=0, tiled=True)]
    unnamed x20 -> x5, local copies, waits for them, and re-layouts: 11.1 us -> 41 us
    dot_general x12 -> x0, matrix products: 26.9 us -> none  [the longest x1 7.31 us: expert_rows(): lax.dot_general(dys, wd, (((1,), (1,)), ((), ())), preferred_element_type...]
    all_gather x1 -> x0, blocking collectives: 9.62 us -> none  [per_device(): lax.all_gather(meta, 'dp', axis=0, tiled=True)]
  transfers between devices with their start and end apart: 3 -> 0, of which waited for: 3 -> 0; matrix products, arithmetic and copies ran while one was open for 4% -> 0% of each run, Pallas kernels for 0% -> 0%
where the time goes in v1:
time: 103 us; the launch traced here: 102 us
  Pallas kernels  59.1 us (57%)
  local copies, waits for them, and re-layouts  42.6 us (41%)
    pallas_call x1, Pallas kernels, per_device(): pl.pallas_call(functools.partial(kernel, n_dp, n_exp), out_shape=jax.Shap...  59.1 us
    unnamed x5, local copies, waits for them, and re-layouts  41 us

profile of v1, /device:TPU:0, one launch (start us, length us, event | category | flops | bytes accessed | tf_op | source)
XLA Modules:
  0.0 101.7 jit_solution(17583642499586748055)
XLA Ops:
  0.0 1.5 %copy.10.routes = s32[256,2]{1,0:T(8,128)} copy(s32[256,2]{0,1:T(2,128)} %param.11) | data formatting | bytes 4096 | tf_op args[2]
  1.5 1.5 %copy.11.codes = s32[256,2]{1,0:T(8,128)} copy(s32[256,2]{0,1:T(2,128)} %param.12) | data formatting | bytes 4096 | tf_op args[3]
  2.9 2.3 %copy.14.proj_hidden = bf16[1600,192]{1,0:T(8,128)(2,1)} copy(bf16[1600,192]{0,1:T(8,128)(2,1)} %param.17) | data formatting | bytes 1228800 | tf_op args[8]
  5.2 17.9 %copy.12.w_gate = bf16[1,4096,1600]{2,1,0:T(8,128)(2,1)} copy(bf16[1,4096,1600]{1,2,0:T(8,128)(2,1)} %param.13) | data formatting | bytes 26214400 | tf_op args[4]
  23.1 17.9 %copy.13.w_up = bf16[1,4096,1600]{2,1,0:T(8,128)(2,1)} copy(bf16[1,4096,1600]{1,2,0:T(8,128)(2,1)} %param.14) | data formatting | bytes 26214400 | tf_op args[5]
  41.0 59.1 %shard_map.91 = f32[4,48,64]{2,1,0:T(8,128)} custom-call(bf16[256,512]{1,0:T(8,128)(2,1)} %tokens.1, bf16[256,512]{1,0:T(8,128)(2,1)} %grads.1, s32[256,2]{1,0:T(8,128)} %copy.10.routes, s32[256,2]{1,0:T(8,128)} %copy.11.codes, bf16[1,4096,1600]{2,1,0:T(8,128)(2,1)} %copy.12.w_gate, bf16[1,4096,1600]{2,1,0:T(8,128)(2,1)} %copy.13.w_up, ...), custom_call_target="tpu_custom_call" | custom-call | tf_op jit(solution)/shard_map/pallas_call | solution.py:289
  100.1 1.6 %reshape.4 = f32[4,1,3072]{2,1,0:T(1,128)} reshape(f32[4,48,64]{2,1,0:T(8,128)} %shard_map.91) | data formatting | bytes 98304 | tf_op jit(solution)/shard_map/reshape | solution.py:319

commit v2 on v1

--- a/solution.py
+++ b/solution.py
@@ -9,7 +9,7 @@
 from jax.sharding import PartitionSpec as P
 
 MESH = pl.DeviceIdType.MESH
-TILE = 256
+TILE = 400
 LAG = 3
 
 
@@ -23,12 +23,12 @@
 
 def kernel(
     n_dp, n_exp, tokens, grads, routes, codes, w_gate, w_up, w_down, proj_in, proj_hidden, out,
-    packed, slots, gate_w, up_w, down_w, gate, upper, back, in_sum, out_sum, hid_sum, weight_rows, parts, arrived,
+    packed, slots, gate_w, up_w, down_w, gate, upper, back, in_sum, out_sum, hid_sum, squeezed, other, weight_rows, parts, arrived,
     load_sem, send_one, recv_one, send_two, recv_two, recv_three, send_row, recv_row, send_part, recv_part,
 ):
     rows, chunk = tokens.shape
     cap = packed.shape[1]
-    hidden = gate.shape[1]
+    hidden = gate.shape[0]
     rank = proj_in.shape[1] // 2
     side = math.isqrt(n_dp)
     units = 2 * n_exp
@@ -50,11 +50,8 @@
 
     def weight_copy(which, j):
         span = pl.ds(pl.multiple_of(j * chunk, chunk), chunk)
-        if which == 0:
-            return pltpu.make_async_copy(w_gate.at[0, span, :], gate_w.at[j], load_sem.at[0, j])
-        if which == 1:
-            return pltpu.make_async_copy(w_up.at[0, span, :], up_w.at[j], load_sem.at[1, j])
-        return pltpu.make_async_copy(w_down.at[0, :, span], down_w.at[j], load_sem.at[2, j])
+        source, target = ((w_gate, gate_w), (w_up, up_w), (w_down, down_w))[which]
+        return pltpu.make_async_copy(source.at[0, :, span], target.at[j], load_sem.at[which, j])
 
     def load_x(k, carry):
         j = swapped(mine, k, n_exp)
@@ -69,18 +66,17 @@
     lax.fori_loop(0, n_exp, load_x, 0)
     lax.fori_loop(0, n_exp, load_dy, 0)
 
-    lanes = max(128, n_exp)
-    experts = lax.broadcasted_iota(jnp.int32, (rows, lanes), 1)
-    first, second = routes[:, 0:1], routes[:, 1:2]
+    depth = max(16, n_exp)
+    experts = lax.broadcasted_iota(jnp.int32, (depth, rows), 0)
+    first, second = routes[0:1, :], routes[1:2, :]
     hit = jnp.where((first == experts) | (second == experts), 1.0, 0.0)
     earlier = jnp.where(
-        lax.broadcasted_iota(jnp.int32, (rows, rows), 1) < lax.broadcasted_iota(jnp.int32, (rows, rows), 0), 1.0, 0.0
+        lax.broadcasted_iota(jnp.int32, (rows, rows), 0) < lax.broadcasted_iota(jnp.int32, (rows, rows), 1), 1.0, 0.0
     )
     place = jnp.dot(
-        earlier.astype(jnp.bfloat16), hit.astype(jnp.bfloat16), preferred_element_type=jnp.float32
-    )
-    key = jnp.where(hit > 0.5, place, -1.0)
-    keys = key.T
+        hit.astype(jnp.bfloat16), earlier.astype(jnp.bfloat16), preferred_element_type=jnp.float32
+    )
+    keys = jnp.where(hit > 0.5, place, -1.0)
     slot_ids = lax.broadcasted_iota(jnp.int32, (cap, rows), 0).astype(jnp.float32)
     picks = jnp.concatenate(
         [jnp.where(keys[e : e + 1, :] == slot_ids, 1.0, 0.0).astype(jnp.bfloat16) for e in range(n_exp)], axis=0
@@ -90,11 +86,12 @@
         packed[a * n_exp : (a + 1) * n_exp] = values.reshape(n_exp, cap, chunk)
         slots[a * n_exp + mine, seq] = packed[a * n_exp + mine]
 
-    own_key = jnp.sum(jnp.where(experts == mine, key, 0.0), axis=1, keepdims=True)
-    own_code = jnp.where(first == mine, codes[:, 0:1], 0) + jnp.where(second == mine, codes[:, 1:2], 0)
-    slot_lanes = lax.broadcasted_iota(jnp.int32, (rows, 128), 1).astype(jnp.float32)
+    own_key = jnp.sum(jnp.where(experts == mine, keys, 0.0), axis=0, keepdims=True)
+    own_code = jnp.where(first == mine, codes[0:1, :], 0) + jnp.where(second == mine, codes[1:2, :], 0)
     own_weight = own_code.astype(jnp.float32) / 4096.0
-    row = jnp.sum(jnp.where(own_key == slot_lanes, own_weight, 0.0), axis=0, keepdims=True)
+    column = jnp.sum(jnp.where(own_key == slot_ids, own_weight, 0.0), axis=1, keepdims=True)
+    diagonal = lax.broadcasted_iota(jnp.int32, (cap, 128), 0) == lax.broadcasted_iota(jnp.int32, (cap, 128), 1)
+    row = jnp.sum(jnp.where(diagonal, column, 0.0), axis=0, keepdims=True)
     weight_rows[seq] = jnp.broadcast_to(row, (8, 128))
 
     pl.semaphore_wait(barrier, n_dp - 1 + n_exp - 1)
@@ -153,8 +150,7 @@
             for to in two:
                 send_block(slots.at[at, source], slots.at[at, source], send_two, recv_three.at[at], to, mine)
 
-    def tiles():
-        return [(n, min(TILE, hidden - n)) for n in range(0, hidden, TILE)]
+    tiles = [slice(n, min(n + TILE, hidden)) for n in range(0, hidden, TILE)]
 
     def stage_three(unit):
         a, k, at = split(unit)
@@ -168,40 +164,36 @@
             weight_copy(1, j).wait()
             block = slots[at].reshape(total_rows, chunk)
             in_sum[...] += jnp.dot(block, proj_in[span, :], preferred_element_type=jnp.float32)
-            for n, width in tiles():
-                cols = slice(n, n + width)
-                gate[:, cols] += jnp.dot(block, gate_w[j, :, cols], preferred_element_type=jnp.float32)
-                upper[:, cols] += jnp.dot(block, up_w[j, :, cols], preferred_element_type=jnp.float32)
+            turned = block.T
+            for part in tiles:
+                gate[part] += jnp.dot(gate_w[j, part, :], turned, preferred_element_type=jnp.float32)
+                upper[part] += jnp.dot(up_w[j, part, :], turned, preferred_element_type=jnp.float32)
 
         @pl.when(a == 1)
         def _():
             weight_copy(2, j).wait()
             block = slots[at].reshape(total_rows, chunk)
             out_sum[...] += jnp.dot(block, proj_in[span, :], preferred_element_type=jnp.float32)
-            for n, width in tiles():
-                cols = slice(n, n + width)
-                back[:, cols] += lax.dot_general(
-                    block, down_w[j, cols, :], (((1,), (1,)), ((), ())), preferred_element_type=jnp.float32
-                )
+            turned = block.T
+            for part in tiles:
+                back[part] += jnp.dot(down_w[j, part, :], turned, preferred_element_type=jnp.float32)
 
         @pl.when(unit == n_exp - 1)
         def _():
-            for n, width in tiles():
-                cols = slice(n, n + width)
-                g, u = gate[:, cols], upper[:, cols]
+            for part in tiles:
+                g, u = gate[part], upper[part]
                 sig = jax.nn.sigmoid(g)
                 act = g * sig
-                hid_sum[...] += jnp.dot(
-                    (act * u).astype(jnp.bfloat16), proj_hidden[cols, :rank], preferred_element_type=jnp.float32
-                )
-                gate[:, cols] = act
-                upper[:, cols] = u * sig * (1.0 + g * (1.0 - sig))
+                gate[part] = act
+                upper[part] = u * sig * (1.0 + g * (1.0 - sig))
+                squeezed[part] = (act * u).astype(jnp.bfloat16)
+            hid_sum[...] = jnp.dot(proj_hidden[:rank], squeezed[...], preferred_element_type=jnp.float32)
 
     lax.fori_loop(1, n_exp, send_out(0), 0)
     for step in range(1, n_dp):
         send_block(weight_rows.at[seq], weight_rows.at[seq], send_row, recv_row, at_seq(step), mine)
     lax.fori_loop(1, n_exp, send_out(1), 0)
-    for ref in (gate, upper, back, in_sum, out_sum, hid_sum):
+    for ref in (gate, upper, back, in_sum, out_sum):
         ref[...] = jnp.zeros_like(ref)
 
     def body(step, carry):
@@ -213,48 +205,33 @@
     lax.fori_loop(0, units + LAG, body, 0)
 
     wait_for(weight_rows.at[pl.ds(0, n_dp - 1)], recv_row)
-    diagonal = lax.broadcasted_iota(jnp.int32, (cap, 128), 0) == lax.broadcasted_iota(jnp.int32, (cap, 128), 1)
-    weight = jnp.concatenate(
-        [
-            jnp.sum(jnp.where(diagonal, weight_rows[s, 0:1, :], 0.0), axis=1, keepdims=True)
-            for s in range(n_dp)
-        ],
-        axis=0,
-    )
-    gate_proj = jnp.zeros((total_rows, rank), jnp.float32)
-    up_proj = jnp.zeros((total_rows, rank), jnp.float32)
-    for n, width in tiles():
-        cols = slice(n, n + width)
-        scaled = back[:, cols] * weight
-        up_proj += jnp.dot(
-            (scaled * gate[:, cols]).astype(jnp.bfloat16), proj_hidden[cols, 2 * rank :],
-            preferred_element_type=jnp.float32,
-        )
-        gate_proj += jnp.dot(
-            (scaled * upper[:, cols]).astype(jnp.bfloat16), proj_hidden[cols, rank : 2 * rank],
-            preferred_element_type=jnp.float32,
-        )
-    in_proj = in_sum[:, :rank]
-    out_proj = out_sum[:, rank:] * weight
-    hid_proj = hid_sum[...]
+    weight = jnp.concatenate([weight_rows[s, 0:1, :cap] for s in range(n_dp)], axis=1)
+    for part in tiles:
+        scaled = back[part] * weight
+        squeezed[part] = (scaled * gate[part]).astype(jnp.bfloat16)
+        other[part] = (scaled * upper[part]).astype(jnp.bfloat16)
+    up_proj = jnp.dot(proj_hidden[2 * rank :], squeezed[...], preferred_element_type=jnp.float32)
+    gate_proj = jnp.dot(proj_hidden[rank : 2 * rank], other[...], preferred_element_type=jnp.float32)
+    in_proj = in_sum[...].T[:rank]
+    out_proj = out_sum[...].T[rank:] * weight
     share = 3 * rank // n_dp
+
+    shape = (n_dp * rank, total_rows)
+    same = lax.div(lax.broadcasted_iota(jnp.int32, shape, 0), rank) == lax.div(
+        lax.broadcasted_iota(jnp.int32, shape, 1), cap
+    )
 
     def product(left, right):
         return lax.dot_general(
-            left, right, (((0,), (0,)), ((), ())),
+            left, right, (((1,), (1,)), ((), ())),
             preferred_element_type=jnp.float32, precision=lax.Precision.HIGHEST,
         )
 
+    left_in = jnp.where(same, jnp.concatenate([in_proj] * n_dp, axis=0), 0.0)
+    left_hid = jnp.where(same, jnp.concatenate([hid_sum[...]] * n_dp, axis=0), 0.0)
+    products = (product(left_in, gate_proj), product(left_in, up_proj), product(left_hid, out_proj))
     for s in range(n_dp):
-        part = slice(s * cap, (s + 1) * cap)
-        stacked = jnp.concatenate(
-            [
-                product(in_proj[part], gate_proj[part]),
-                product(in_proj[part], up_proj[part]),
-                product(hid_proj[part], out_proj[part]),
-            ],
-            axis=0,
-        )
+        stacked = jnp.concatenate([value[s * rank : (s + 1) * rank] for value in products], axis=0)
         for d in range(n_dp):
             parts[d, s] = stacked[d * share : (d + 1) * share]
     for step in range(1, n_dp):
@@ -294,15 +271,17 @@
         scratch_shapes=[
             pltpu.VMEM((2 * n_exp, cap, chunk), bf16),
             pltpu.VMEM((2 * n_exp, n_dp, cap, chunk), bf16),
-            pltpu.VMEM((n_exp, chunk, hidden), bf16),
-            pltpu.VMEM((n_exp, chunk, hidden), bf16),
             pltpu.VMEM((n_exp, hidden, chunk), bf16),
-            pltpu.VMEM((total, hidden), f32),
-            pltpu.VMEM((total, hidden), f32),
-            pltpu.VMEM((total, hidden), f32),
+            pltpu.VMEM((n_exp, hidden, chunk), bf16),
+            pltpu.VMEM((n_exp, hidden, chunk), bf16),
+            pltpu.VMEM((hidden, total), f32),
+            pltpu.VMEM((hidden, total), f32),
+            pltpu.VMEM((hidden, total), f32),
             pltpu.VMEM((total, 2 * rank), f32),
             pltpu.VMEM((total, 2 * rank), f32),
-            pltpu.VMEM((total, rank), f32),
+            pltpu.VMEM((rank, total), f32),
+            pltpu.VMEM((hidden, total), bf16),
+            pltpu.VMEM((hidden, total), bf16),
             pltpu.VMEM((n_dp, 8, 128), f32),
             pltpu.VMEM((n_dp, n_dp, share, rank), f32),
             pltpu.VMEM((n_dp, n_dp, share, rank), f32),
@@ -315,7 +294,10 @@
         compiler_params=pltpu.CompilerParams(
             collective_id=0, has_side_effects=True, vmem_limit_bytes=60 * 1024 * 1024
         ),
-    )(tokens, out_grads, routes, gate_codes, w_gate, w_up, w_down, proj_in, proj_hidden)
+    )(
+        tokens, out_grads, routes.T, gate_codes.T, jnp.swapaxes(w_gate, 1, 2), jnp.swapaxes(w_up, 1, 2), w_down,
+        proj_in, proj_hidden.T,
+    )
     return result.reshape(n_dp, 1, share * rank)
 
 

time: 103 us -> 60.3 us (0.59); the launches traced: 102 us -> 60.1 us
  local copies, waits for them, and re-layouts: 42.6 us -> 1.63 us
    unnamed x5 -> x0, local copies, waits for them, and re-layouts: 41 us -> none
where the time goes in v2:
time: 60.3 us; the launch traced here: 60.1 us
  Pallas kernels  58.5 us (97%)
  local copies, waits for them, and re-layouts  1.63 us (3%)
    pallas_call x1, Pallas kernels, per_device(): pl.pallas_call(functools.partial(kernel, n_dp, n_exp), out_shape=jax.Shap...  58.5 us
    reshape x1, local copies, waits for them, and re-layouts, per_device(): return result.reshape(n_dp, 1, share * rank)  1.63 us

profile of v2, /device:TPU:0, one launch (start us, length us, event | category | flops | bytes accessed | tf_op | source)
XLA Modules:
  0.0 60.1 jit_solution(8114594220461328321)
XLA Ops:
  0.0 58.5 %shard_map.91 = f32[4,48,64]{2,1,0:T(8,128)} custom-call(bf16[256,512]{1,0:T(8,128)(2,1)} %tokens.1, bf16[256,512]{1,0:T(8,128)(2,1)} %grads.1, s32[2,256]{1,0:T(2,128)} %bitcast.8, s32[2,256]{1,0:T(2,128)} %bitcast.9, bf16[1,1600,4096]{2,1,0:T(8,128)(2,1)} %bitcast.5, bf16[1,1600,4096]{2,1,0:T(8,128)(2,1)} %bitcast.6, bf16[1,1600,4096]{2,1,0:T(8,128)(2,1)} %w_down.1, ...), custom_call_target="tpu_custom_call" | custom-call | tf_op jit(solution)/shard_map/pallas_call | solution.py:266
  58.5 1.6 %reshape.4 = f32[4,1,3072]{2,1,0:T(1,128)} reshape(f32[4,48,64]{2,1,0:T(8,128)} %shard_map.91) | data formatting | bytes 98304 | tf_op jit(solution)/shard_map/reshape | solution.py:301

commit v3 on v2

--- a/solution.py
+++ b/solution.py
@@ -10,7 +10,10 @@
 
 MESH = pl.DeviceIdType.MESH
 TILE = 400
-LAG = 3
+AHEAD = 8
+LOADS = 4
+RELAY = 2
+LAG = 4
 
 
 def swapped(a, b, count):
@@ -22,14 +25,14 @@
 
 
 def kernel(
-    n_dp, n_exp, tokens, grads, routes, codes, w_gate, w_up, w_down, proj_in, proj_hidden, out,
-    packed, slots, gate_w, up_w, down_w, gate, upper, back, in_sum, out_sum, hid_sum, squeezed, other, weight_rows, parts, arrived,
-    load_sem, send_one, recv_one, send_two, recv_two, recv_three, send_row, recv_row, send_part, recv_part,
+    n_dp, n_exp, tokens, grads, routes, codes, w_gate, w_up, w_down, proj_in_hbm, proj_hidden_hbm, out,
+    packed, slots, gate_w, up_w, down_w, gate, upper, back, in_sum, out_sum, hid_sum, squeezed, other, proj_in, proj_hidden, weight_rows, parts, arrived,
+    load_sem, proj_sem, send_one, recv_one, send_two, recv_two, recv_three, send_row, recv_row, send_part, recv_part,
 ):
     rows, chunk = tokens.shape
     cap = packed.shape[1]
     hidden = gate.shape[0]
-    rank = proj_in.shape[1] // 2
+    rank = proj_in_hbm.shape[1] // 2
     side = math.isqrt(n_dp)
     units = 2 * n_exp
     total_rows = n_dp * cap
@@ -53,18 +56,35 @@
         source, target = ((w_gate, gate_w), (w_up, up_w), (w_down, down_w))[which]
         return pltpu.make_async_copy(source.at[0, :, span], target.at[j], load_sem.at[which, j])
 
-    def load_x(k, carry):
+    projections = (
+        pltpu.make_async_copy(proj_in_hbm, proj_in, proj_sem.at[0]),
+        pltpu.make_async_copy(proj_hidden_hbm, proj_hidden, proj_sem.at[1]),
+    )
+
+    def split(unit):
+        base, size, edge = 0, 2, 4
+        while edge < units:
+            past = lax.div(lax.div(unit, edge) + units, units + 1)
+            base = base + past * (edge if edge == 4 else edge // 2)
+            size = size + past * (0 if edge == 4 else edge // 4)
+            edge *= 2
+        within = unit - base
+        a = lax.div(within, size)
+        k = lax.rem(within, size) + size * lax.div(lax.div(unit, 4) + units, units + 1)
+        return a, k, a * n_exp + swapped(mine, k, n_exp)
+
+    def load(unit):
+        a, k, _ = split(unit)
         j = swapped(mine, k, n_exp)
-        weight_copy(0, j).start()
-        weight_copy(1, j).start()
-        return carry
-
-    def load_dy(k, carry):
-        weight_copy(2, swapped(mine, k, n_exp)).start()
-        return carry
-
-    lax.fori_loop(0, n_exp, load_x, 0)
-    lax.fori_loop(0, n_exp, load_dy, 0)
+
+        @pl.when(a == 0)
+        def _():
+            weight_copy(0, j).start()
+            weight_copy(1, j).start()
+
+        @pl.when(a == 1)
+        def _():
+            weight_copy(2, j).start()
 
     depth = max(16, n_exp)
     experts = lax.broadcasted_iota(jnp.int32, (depth, rows), 0)
@@ -115,19 +135,16 @@
             two.append(along_y + odd * (along_x - along_y))
         return one, two
 
-    def split(unit):
-        a, k = lax.div(unit, n_exp), lax.rem(unit, n_exp)
-        return a, k, a * n_exp + swapped(mine, k, n_exp)
-
-    def send_out(a):
-        def body(k, carry):
+    def send_out(unit):
+        a, k, _ = split(unit)
+
+        @pl.when(k > 0)
+        def _():
             to = swapped(mine, k, n_exp)
             send_block(
                 packed.at[a * n_exp + to], slots.at[a * n_exp + mine, seq],
                 send_one, recv_one.at[a * n_exp + mine], seq, to,
             )
-            return carry
-        return body
 
     def stage_one(unit):
         a, k, at = split(unit)
@@ -178,7 +195,7 @@
             for part in tiles:
                 back[part] += jnp.dot(down_w[j, part, :], turned, preferred_element_type=jnp.float32)
 
-        @pl.when(unit == n_exp - 1)
+        @pl.when(unit == units - n_exp // 2 - 1)
         def _():
             for part in tiles:
                 g, u = gate[part], upper[part]
@@ -189,20 +206,32 @@
                 squeezed[part] = (act * u).astype(jnp.bfloat16)
             hid_sum[...] = jnp.dot(proj_hidden[:rank], squeezed[...], preferred_element_type=jnp.float32)
 
-    lax.fori_loop(1, n_exp, send_out(0), 0)
+    def loop(low, high, function):
+        def body(index, carry):
+            function(index)
+            return carry
+
+        lax.fori_loop(low, high, body, 0)
+
+    loop(0, AHEAD, send_out)
     for step in range(1, n_dp):
         send_block(weight_rows.at[seq], weight_rows.at[seq], send_row, recv_row, at_seq(step), mine)
-    lax.fori_loop(1, n_exp, send_out(1), 0)
+    for copy in projections:
+        copy.start()
+    loop(0, LOADS, load)
     for ref in (gate, upper, back, in_sum, out_sum):
         ref[...] = jnp.zeros_like(ref)
-
-    def body(step, carry):
+    for copy in projections:
+        copy.wait()
+
+    def step_of(step):
         pl.when(step < units)(lambda: stage_one(step))
-        pl.when((step >= 1) & (step <= units))(lambda: stage_two(step - 1))
+        pl.when(step < units - AHEAD)(lambda: send_out(step + AHEAD))
+        pl.when((step >= RELAY) & (step < units + RELAY))(lambda: stage_two(step - RELAY))
+        pl.when(step < units - LOADS)(lambda: load(step + LOADS))
         pl.when(step >= LAG)(lambda: stage_three(step - LAG))
-        return carry
-
-    lax.fori_loop(0, units + LAG, body, 0)
+
+    loop(0, units + LAG, step_of)
 
     wait_for(weight_rows.at[pl.ds(0, n_dp - 1)], recv_row)
     weight = jnp.concatenate([weight_rows[s, 0:1, :cap] for s in range(n_dp)], axis=1)
@@ -233,7 +262,8 @@
     for s in range(n_dp):
         stacked = jnp.concatenate([value[s * rank : (s + 1) * rank] for value in products], axis=0)
         for d in range(n_dp):
-            parts[d, s] = stacked[d * share : (d + 1) * share]
+            low, mid, high = d * share, d * share + share // 2, (d + 1) * share
+            parts[d, s] = jnp.concatenate([stacked[low:mid], stacked[mid:high]], axis=1)
     for step in range(1, n_dp):
         to = at_seq(step)
         send_block(parts.at[to], arrived.at[seq], send_part, recv_part, to, mine)
@@ -242,7 +272,7 @@
     result = arrived[0]
     for s in range(1, n_dp):
         result += arrived[s]
-    out[...] = result
+    out[...] = jnp.concatenate([result[:, :, :rank], result[:, :, rank:]], axis=1)
 
     wait_for(packed.at[pl.ds(0, 2 * (n_exp - 1))], send_one)
     wait_for(slots.at[:, pl.ds(0, n_dp - 1)], send_two)
@@ -266,7 +296,7 @@
     result = pl.pallas_call(
         functools.partial(kernel, n_dp, n_exp),
         out_shape=jax.ShapeDtypeStruct((n_dp, share, rank), f32),
-        in_specs=[vmem, vmem, vmem, vmem, hbm, hbm, hbm, vmem, vmem],
+        in_specs=[vmem, vmem, vmem, vmem, hbm, hbm, hbm, hbm, hbm],
         out_specs=vmem,
         scratch_shapes=[
             pltpu.VMEM((2 * n_exp, cap, chunk), bf16),
@@ -282,10 +312,13 @@
             pltpu.VMEM((rank, total), f32),
             pltpu.VMEM((hidden, total), bf16),
             pltpu.VMEM((hidden, total), bf16),
+            pltpu.VMEM(proj_in.shape, bf16),
+            pltpu.VMEM(proj_hidden.shape[::-1], bf16),
             pltpu.VMEM((n_dp, 8, 128), f32),
-            pltpu.VMEM((n_dp, n_dp, share, rank), f32),
-            pltpu.VMEM((n_dp, n_dp, share, rank), f32),
+            pltpu.VMEM((n_dp, n_dp, share // 2, 2 * rank), f32),
+            pltpu.VMEM((n_dp, n_dp, share // 2, 2 * rank), f32),
             dma((3, n_exp)),
+            dma((2,)),
             dma, dma((2 * n_exp,)),
             dma, dma((2 * n_exp,)), dma((2 * n_exp,)),
             dma, dma,

time: 60.3 us -> 55.1 us (0.914)
  Pallas kernels: 58.5 us -> 53.3 us
    pallas_call x1, Pallas kernels: 58.5 us -> 53.3 us  [per_device(): pl.pallas_call(functools.partial(kernel, n_dp, n_exp), out_shape=jax.Shap...]
where the time goes in v3:
time: 55.1 us; the launch traced here: 54.9 us
  Pallas kernels  53.3 us (97%)
  local copies, waits for them, and re-layouts  1.63 us (3%)
    pallas_call x1, Pallas kernels, per_device(): pl.pallas_call(functools.partial(kernel, n_dp, n_exp), out_shape=jax.Shap...  53.3 us
    reshape x1, local copies, waits for them, and re-layouts, per_device(): return result.reshape(n_dp, 1, share * rank)  1.63 us

profile of v3, /device:TPU:0, one launch (start us, length us, event | category | flops | bytes accessed | tf_op | source)
XLA Modules:
  0.0 54.9 jit_solution(8051031834579367167)
XLA Ops:
  0.0 53.3 %shard_map.91 = f32[4,48,64]{2,1,0:T(8,128)} custom-call(bf16[256,512]{1,0:T(8,128)(2,1)} %tokens.1, bf16[256,512]{1,0:T(8,128)(2,1)} %grads.1, s32[2,256]{1,0:T(2,128)} %bitcast.8, s32[2,256]{1,0:T(2,128)} %bitcast.9, bf16[1,1600,4096]{2,1,0:T(8,128)(2,1)} %bitcast.5, bf16[1,1600,4096]{2,1,0:T(8,128)(2,1)} %bitcast.6, bf16[1,1600,4096]{2,1,0:T(8,128)(2,1)} %w_down.1, ...), custom_call_target="tpu_custom_call" | custom-call | tf_op jit(solution)/shard_map/pallas_call | solution.py:296
  53.3 1.6 %reshape.4 = f32[4,1,3072]{2,1,0:T(1,128)} reshape(f32[4,48,64]{2,1,0:T(8,128)} %shard_map.91) | data formatting | bytes 98304 | tf_op jit(solution)/shard_map/reshape | solution.py:334

commit v4 on v3

--- a/solution.py
+++ b/solution.py
@@ -12,8 +12,8 @@
 TILE = 400
 AHEAD = 8
 LOADS = 4
-RELAY = 2
-LAG = 4
+RELAY = 3
+LAG = 5
 
 
 def swapped(a, b, count):
@@ -26,7 +26,7 @@
 
 def kernel(
     n_dp, n_exp, tokens, grads, routes, codes, w_gate, w_up, w_down, proj_in_hbm, proj_hidden_hbm, out,
-    packed, slots, gate_w, up_w, down_w, gate, upper, back, in_sum, out_sum, hid_sum, squeezed, other, proj_in, proj_hidden, weight_rows, parts, arrived,
+    packed, slots, gate_w, up_w, down_w, gate, upper, back, in_sum, out_sum, squeezed, other, turned_in, turned_hid, left_in, left_hid, proj_in, proj_hidden, weight_rows, whole_parts, parts, arrived,
     load_sem, proj_sem, send_one, recv_one, send_two, recv_two, recv_three, send_row, recv_row, send_part, recv_part,
 ):
     rows, chunk = tokens.shape
@@ -169,6 +169,10 @@
 
     tiles = [slice(n, min(n + TILE, hidden)) for n in range(0, hidden, TILE)]
 
+    def halves(value):
+        high = value.astype(jnp.bfloat16)
+        return high, (value - high.astype(jnp.float32)).astype(jnp.bfloat16)
+
     def stage_three(unit):
         a, k, at = split(unit)
         j = swapped(mine, k, n_exp)
@@ -204,7 +208,26 @@
                 gate[part] = act
                 upper[part] = u * sig * (1.0 + g * (1.0 - sig))
                 squeezed[part] = (act * u).astype(jnp.bfloat16)
-            hid_sum[...] = jnp.dot(proj_hidden[:rank], squeezed[...], preferred_element_type=jnp.float32)
+            hid_proj = jnp.dot(proj_hidden[:rank], squeezed[...], preferred_element_type=jnp.float32)
+            in_proj = in_sum[...].T[:rank]
+            for piece in range(turned_in.shape[0]):
+                lanes = slice(piece * turned_in.shape[2], (piece + 1) * turned_in.shape[2])
+                turned_in[piece] = in_proj[:, lanes]
+                turned_hid[piece] = hid_proj[:, lanes]
+            half = rank // 2
+            shape = (n_dp * rank, total_rows)
+            row_seq = lax.div(lax.rem(lax.broadcasted_iota(jnp.int32, shape, 0), n_dp * half), half)
+            same = row_seq == lax.div(lax.broadcasted_iota(jnp.int32, shape, 1), cap)
+            for target, source in ((left_in, turned_in), (left_hid, turned_hid)):
+                even, odd = (
+                    jnp.concatenate(
+                        [source[piece, pl.ds(parity, half, stride=2), :] for piece in range(source.shape[0])], axis=1
+                    )
+                    for parity in range(2)
+                )
+                spread = jnp.concatenate([even] * n_dp + [odd] * n_dp, axis=0)
+                high, low = halves(jnp.where(same, spread, 0.0))
+                target[...] = jnp.concatenate([high, low, high], axis=1)
 
     def loop(low, high, function):
         def body(index, carry):
@@ -241,38 +264,34 @@
         other[part] = (scaled * upper[part]).astype(jnp.bfloat16)
     up_proj = jnp.dot(proj_hidden[2 * rank :], squeezed[...], preferred_element_type=jnp.float32)
     gate_proj = jnp.dot(proj_hidden[rank : 2 * rank], other[...], preferred_element_type=jnp.float32)
-    in_proj = in_sum[...].T[:rank]
     out_proj = out_sum[...].T[rank:] * weight
-    share = 3 * rank // n_dp
-
-    shape = (n_dp * rank, total_rows)
-    same = lax.div(lax.broadcasted_iota(jnp.int32, shape, 0), rank) == lax.div(
-        lax.broadcasted_iota(jnp.int32, shape, 1), cap
-    )
+    half = rank // 2
+    share = 3 * half // n_dp
 
     def product(left, right):
-        return lax.dot_general(
-            left, right, (((1,), (1,)), ((), ())),
-            preferred_element_type=jnp.float32, precision=lax.Precision.HIGHEST,
+        high, low = halves(right)
+        value = lax.dot_general(
+            left[...], jnp.concatenate([high, high, low], axis=1), (((1,), (1,)), ((), ())),
+            preferred_element_type=jnp.float32,
         )
-
-    left_in = jnp.where(same, jnp.concatenate([in_proj] * n_dp, axis=0), 0.0)
-    left_hid = jnp.where(same, jnp.concatenate([hid_sum[...]] * n_dp, axis=0), 0.0)
+        return jnp.concatenate([value[: n_dp * half], value[n_dp * half :]], axis=1)
+
     products = (product(left_in, gate_proj), product(left_in, up_proj), product(left_hid, out_proj))
-    for s in range(n_dp):
-        stacked = jnp.concatenate([value[s * rank : (s + 1) * rank] for value in products], axis=0)
-        for d in range(n_dp):
-            low, mid, high = d * share, d * share + share // 2, (d + 1) * share
-            parts[d, s] = jnp.concatenate([stacked[low:mid], stacked[mid:high]], axis=1)
+    stacked = [
+        jnp.concatenate([value[s * half : (s + 1) * half] for value in products], axis=0) for s in range(n_dp)
+    ]
+    for d in range(n_dp):
+        block = jnp.concatenate([value[d * share : (d + 1) * share] for value in stacked], axis=0)
+        whole_parts[d] = block
+        parts[d] = block.astype(jnp.bfloat16)
     for step in range(1, n_dp):
         to = at_seq(step)
         send_block(parts.at[to], arrived.at[seq], send_part, recv_part, to, mine)
-    arrived[seq] = parts[seq]
     wait_for(arrived.at[pl.ds(0, n_dp - 1)], recv_part)
-    result = arrived[0]
-    for s in range(1, n_dp):
-        result += arrived[s]
-    out[...] = jnp.concatenate([result[:, :, :rank], result[:, :, rank:]], axis=1)
+    result = whole_parts[seq]
+    for step in range(1, n_dp):
+        result += arrived[at_seq(step)].astype(jnp.float32)
+    out[...] = result
 
     wait_for(packed.at[pl.ds(0, 2 * (n_exp - 1))], send_one)
     wait_for(slots.at[:, pl.ds(0, n_dp - 1)], send_two)
@@ -289,13 +308,14 @@
     rank = proj_in.shape[1] // 2
     share = 3 * rank // n_dp
     total = n_dp * cap
+    lanes = min(128, total)
     vmem = pl.BlockSpec(memory_space=pltpu.VMEM)
     hbm = pl.BlockSpec(memory_space=pl.ANY)
     f32, bf16 = jnp.float32, jnp.bfloat16
     dma = pltpu.SemaphoreType.DMA
     result = pl.pallas_call(
         functools.partial(kernel, n_dp, n_exp),
-        out_shape=jax.ShapeDtypeStruct((n_dp, share, rank), f32),
+        out_shape=jax.ShapeDtypeStruct((3 * rank // 2, 2 * rank), f32),
         in_specs=[vmem, vmem, vmem, vmem, hbm, hbm, hbm, hbm, hbm],
         out_specs=vmem,
         scratch_shapes=[
@@ -309,14 +329,18 @@
             pltpu.VMEM((hidden, total), f32),
             pltpu.VMEM((total, 2 * rank), f32),
             pltpu.VMEM((total, 2 * rank), f32),
-            pltpu.VMEM((rank, total), f32),
             pltpu.VMEM((hidden, total), bf16),
             pltpu.VMEM((hidden, total), bf16),
+            pltpu.VMEM((total // lanes, rank, lanes), f32),
+            pltpu.VMEM((total // lanes, rank, lanes), f32),
+            pltpu.VMEM((n_dp * rank, 3 * total), bf16),
+            pltpu.VMEM((n_dp * rank, 3 * total), bf16),
             pltpu.VMEM(proj_in.shape, bf16),
             pltpu.VMEM(proj_hidden.shape[::-1], bf16),
             pltpu.VMEM((n_dp, 8, 128), f32),
-            pltpu.VMEM((n_dp, n_dp, share // 2, 2 * rank), f32),
-            pltpu.VMEM((n_dp, n_dp, share // 2, 2 * rank), f32),
+            pltpu.VMEM((n_dp, 3 * rank // 2, 2 * rank), f32),
+            pltpu.VMEM((n_dp, 3 * rank // 2, 2 * rank), bf16),
+            pltpu.VMEM((n_dp, 3 * rank // 2, 2 * rank), bf16),
             dma((3, n_exp)),
             dma((2,)),
             dma, dma((2 * n_exp,)),

time: 55.1 us -> 54.6 us (level)
    reshape x1 -> x0, local copies, waits for them, and re-layouts: 1.63 us -> none  [per_device(): return result.reshape(n_dp, 1, share * rank)]
    unnamed x0 -> x1, local copies, waits for them, and re-layouts: none -> 1.42 us
where the time goes in v4:
time: 54.6 us; the launch traced here: 54.4 us
  Pallas kernels  53 us (97%)
  local copies, waits for them, and re-layouts  1.42 us (3%)
    pallas_call x1, Pallas kernels, per_device(): pl.pallas_call(functools.partial(kernel, n_dp, n_exp), out_shape=jax.Shap...  53 us
    unnamed x1, local copies, waits for them, and re-layouts  1.42 us

profile of v4, /device:TPU:0, one launch (start us, length us, event | category | flops | bytes accessed | tf_op | source)
XLA Modules:
  0.0 54.4 jit_solution(787844717047272151)
XLA Ops:
  0.0 53.0 %shard_map.91 = f32[96,128]{1,0:T(8,128)} custom-call(bf16[256,512]{1,0:T(8,128)(2,1)} %tokens.1, bf16[256,512]{1,0:T(8,128)(2,1)} %grads.1, s32[2,256]{1,0:T(2,128)} %bitcast.10, s32[2,256]{1,0:T(2,128)} %bitcast.11, bf16[1,1600,4096]{2,1,0:T(8,128)(2,1)} %bitcast.6, bf16[1,1600,4096]{2,1,0:T(8,128)(2,1)} %bitcast.7, bf16[1,1600,4096]{2,1,0:T(8,128)(2,1)} %w_down.1, ...), custom_call_target="tpu_custom_call" | custom-call | tf_op jit(solution)/shard_map/pallas_call | solution.py:316
  53.0 1.4 %copy.12 = f32[4,1,3072]{2,1,0:T(1,128)} copy(f32[4,1,3072]{2,1,0:T(1,128)} %bitcast.9) | data formatting | bytes 98304

commit v5 on v4

--- a/solution.py
+++ b/solution.py
@@ -10,7 +10,7 @@
 
 MESH = pl.DeviceIdType.MESH
 TILE = 400
-AHEAD = 8
+AHEAD = 12
 LOADS = 4
 RELAY = 3
 LAG = 5
@@ -126,7 +126,7 @@
         pltpu.make_async_copy(ref, ref, sem).wait()
 
     def peers(k):
-        odd = lax.rem(k, 2)
+        odd = lax.rem(k + mine, 2)
         one, two = [], []
         for step in range(1, side):
             along_x = seq_y * side + lax.rem(seq_x + step, side)
@@ -236,7 +236,11 @@
 
         lax.fori_loop(low, high, body, 0)
 
-    loop(0, AHEAD, send_out)
+    stage_one(0)
+    loop(1, 4, send_out)
+    for unit in range(4, 8):
+        send_out(unit)
+        send_out(unit + 4)
     for step in range(1, n_dp):
         send_block(weight_rows.at[seq], weight_rows.at[seq], send_row, recv_row, at_seq(step), mine)
     for copy in projections:
@@ -248,7 +252,7 @@
         copy.wait()
 
     def step_of(step):
-        pl.when(step < units)(lambda: stage_one(step))
+        pl.when((step >= 1) & (step < units))(lambda: stage_one(step))
         pl.when(step < units - AHEAD)(lambda: send_out(step + AHEAD))
         pl.when((step >= RELAY) & (step < units + RELAY))(lambda: stage_two(step - RELAY))
         pl.when(step < units - LOADS)(lambda: load(step + LOADS))

time: 54.6 us -> 53.6 us (0.982)
  Pallas kernels: 53 us -> 52 us
    pallas_call x1, Pallas kernels: 53 us -> 52 us  [per_device(): pl.pallas_call(functools.partial(kernel, n_dp, n_exp), out_shape=jax.Shap...]
where the time goes in v5:
time: 53.6 us; the launch traced here: 53.4 us
  Pallas kernels  52 us (97%)
  local copies, waits for them, and re-layouts  1.42 us (3%)
    pallas_call x1, Pallas kernels, per_device(): pl.pallas_call(functools.partial(kernel, n_dp, n_exp), out_shape=jax.Shap...  52 us
    unnamed x1, local copies, waits for them, and re-layouts  1.42 us

profile of v5, /device:TPU:0, one launch (start us, length us, event | category | flops | bytes accessed | tf_op | source)
XLA Modules:
  0.0 53.4 jit_solution(197781359785630405)
XLA Ops:
  0.0 52.0 %shard_map.91 = f32[96,128]{1,0:T(8,128)} custom-call(bf16[256,512]{1,0:T(8,128)(2,1)} %tokens.1, bf16[256,512]{1,0:T(8,128)(2,1)} %grads.1, s32[2,256]{1,0:T(2,128)} %bitcast.10, s32[2,256]{1,0:T(2,128)} %bitcast.11, bf16[1,1600,4096]{2,1,0:T(8,128)(2,1)} %bitcast.6, bf16[1,1600,4096]{2,1,0:T(8,128)(2,1)} %bitcast.7, bf16[1,1600,4096]{2,1,0:T(8,128)(2,1)} %w_down.1, ...), custom_call_target="tpu_custom_call" | custom-call | tf_op jit(solution)/shard_map/pallas_call | solution.py:320
  52.0 1.4 %copy.12 = f32[4,1,3072]{2,1,0:T(1,128)} copy(f32[4,1,3072]{2,1,0:T(1,128)} %bitcast.9) | data formatting | bytes 98304
